TPU v7x, 512 devices: a whole 4x4x16 slice. The times are simulated.
512 devices in a mesh: row: 16 (over x, y), col: 32 (over z, core).
Axes of the slice: x: 4, y: 4, z: 16, core: 2. Of those that a mesh axis runs over, the one named last changes fastest.
Arguments:
- design: float32 [4096, 122880], P('row', 'col')
- targets: float32 [64, 4096], P(None, 'row')
Outputs:
- solution: float32 [64, 122880], P(None, 'col')
All inputs are finite; a program needn't handle non-finite values.
Results may differ from a plain program's by a relative error of at most 0.0001.
Values sent between devices are 32-bit elements; how exact they have to be, the bound alone decides.
A program may use at most 64 MiB of HBM per device.

v0:
```python
import jax
import jax.numpy as jnp
from jax import lax
from jax.sharding import PartitionSpec as P

ITERS = 2


def local(design, targets):
    highest = lax.Precision.HIGHEST

    def back_product(vector):
        return jnp.dot(vector, design, precision=highest, preferred_element_type=jnp.float32)

    def forward_product(vector):
        return lax.dot_general(
            vector,
            design,
            (((1,), (1,)), ((), ())),
            precision=highest,
            preferred_element_type=jnp.float32,
        )

    def squares(matrix):
        return jnp.sum(matrix * matrix, axis=1)

    def row_norm(left_raw):
        return jnp.sqrt(lax.psum(squares(left_raw), "row"))

    def col_norm(right_full):
        return jnp.sqrt(lax.psum(squares(right_full), "col"))

    def back_step(left_raw):
        u_norm = row_norm(left_raw)
        back_out = lax.psum(back_product(left_raw / u_norm[:, None]), "row")
        return (u_norm, back_out)

    def forward_step(right_raw):
        v_norm = col_norm(right_raw)
        forward_out = lax.psum(forward_product(right_raw / v_norm[:, None]), "col")
        return (v_norm, right_raw / v_norm[:, None], forward_out)

    u_norm, back_out = back_step(targets)
    left_vec = targets / u_norm[:, None]
    v_norm, right_vec, forward_out = forward_step(back_out)
    direction = right_vec
    solution = jnp.zeros_like(right_vec)
    phi_bar = u_norm
    rho_bar = v_norm
    for iteration in range(ITERS):
        final = iteration + 1 == ITERS
        left_raw = forward_out - v_norm[:, None] * left_vec
        if final:
            u_norm = row_norm(left_raw)
        else:
            u_norm, back_out = back_step(left_raw)
            left_vec = left_raw / u_norm[:, None]
            right_raw = back_out - u_norm[:, None] * right_vec
            v_norm, right_vec, forward_out = forward_step(right_raw)
        rho_value = jnp.sqrt(rho_bar * rho_bar + u_norm * u_norm)
        cosine = rho_bar / rho_value
        sine_value = u_norm / rho_value
        phi_value = cosine * phi_bar
        phi_bar = sine_value * phi_bar
        solution = solution + (phi_value / rho_value)[:, None] * direction
        if not final:
            rho_bar = -cosine * v_norm
            direction = right_vec - (sine_value * v_norm / rho_value)[:, None] * direction
    return solution


def solution(mesh):
    in_specs = (P("row", "col"), P(None, "row"))
    out_specs = P(None, "col")
    return jax.shard_map(local, mesh=mesh, in_specs=in_specs, out_specs=out_specs, check_vma=False)
```

profile of v0, /device:TPU:1, one launch (start us, length us, event | category | flops | bytes accessed | tf_op | source)
XLA Modules:
  0.0 839.0 jit_solution(1270484130718466527)
XLA Ops:
  6.5 0.9 multiply_reduce_fusion.4
  7.5 34.3 %psum.63 = f32[64]{0:T(128)S(1)} all-reduce(f32[64]{0:T(128)S(1)} %multiply_reduce_fusion.4), channel_id=1, replica_groups=mesh['row'=16,'col'=32] {'row'}, use_global_device_ids=true, to_apply=%region_1.0 | all-reduce | flops 64 | bytes 512 | tf_op jit(solution)/shard_map/psum | solution.py:28
  41.8 5.6 fusion.1
  47.3 0.0 all-reduce.5.cloned.1.call-update
  47.3 0.0 all-reduce.7.cloned.1.call-start
  47.4 122.1 %all-reduce.5.cloned.1.call-done = f32[64,3840]{1,0:T(8,128)} async-done(((f32[64,3840]{1,0:T(8,128)}), f32[64,3840]{1,0:T(8,128)}) %all-reduce.5.cloned.1.call-update) | async-done | bytes 983056 | tf_op jit(solution)/shard_map/psum | solution.py:35
  169.5 1.4 multiply_reduce_fusion.1
  170.9 48.5 %psum.65 = f32[64]{0:T(128)S(1)} all-reduce(f32[64]{0:T(128)S(1)} %multiply_reduce_fusion.1), channel_id=1, replica_groups=mesh['row'=16,'col'=32] {'col'}, use_global_device_ids=true, to_apply=%region_4.0 | all-reduce | flops 64 | bytes 512 | tf_op jit(solution)/shard_map/psum | solution.py:31
  219.4 6.8 fusion.3
  226.2 0.0 all-reduce.7.cloned.1.call-update
  226.2 0.0 all-reduce.9.cloned.1.call-start
  226.3 181.6 %all-reduce.7.cloned.1.call-done = f32[64,256]{1,0:T(8,128)} async-done(((f32[64,256]{1,0:T(8,128)}), f32[64,256]{1,0:T(8,128)}) %all-reduce.7.cloned.1.call-update) | async-done | bytes 65552 | tf_op jit(solution)/shard_map/psum | solution.py:40
  407.8 1.0 multiply_reduce_fusion.3
  408.9 33.1 %psum.67 = f32[64]{0:T(128)S(1)} all-reduce(f32[64]{0:T(128)S(1)} %get-tuple-element.10), channel_id=1, replica_groups=mesh['row'=16,'col'=32] {'row'}, use_global_device_ids=true, to_apply=%region_7.0 | all-reduce | flops 64 | bytes 512 | tf_op jit(solution)/shard_map/psum | solution.py:28
  442.0 5.5 fusion.2
  447.6 0.0 all-reduce.11.cloned.1.call-start
  447.6 110.7 %all-reduce.9.cloned.1.call-done = f32[64,3840]{1,0:T(8,128)} async-done(((f32[64,3840]{1,0:T(8,128)}), f32[64,3840]{1,0:T(8,128)}) %all-reduce.9.cloned.1.call-update) | async-done | bytes 983056 | tf_op jit(solution)/shard_map/psum | solution.py:35
  558.3 1.5 multiply_reduce_fusion
  559.9 48.7 %psum.69 = f32[64]{0:T(128)S(1)} all-reduce(f32[64]{0:T(128)S(1)} %multiply_reduce_fusion), channel_id=1, replica_groups=mesh['row'=16,'col'=32] {'col'}, use_global_device_ids=true, to_apply=%region_10.0 | all-reduce | flops 64 | bytes 512 | tf_op jit(solution)/shard_map/psum | solution.py:31
  608.5 6.8 fusion
  615.3 181.6 %all-reduce.11.cloned.1.call-done = f32[64,256]{1,0:T(8,128)} async-done(((f32[64,256]{1,0:T(8,128)}), f32[64,256]{1,0:T(8,128)}) %all-reduce.11.cloned.1.call-update) | async-done | bytes 65552 | tf_op jit(solution)/shard_map/psum | solution.py:40
  796.9 1.0 multiply_reduce_fusion.2
  798.0 33.1 %psum.71 = f32[64]{0:T(128)S(1)} all-reduce(f32[64]{0:T(128)S(1)} %multiply_reduce_fusion.2), channel_id=1, replica_groups=mesh['row'=16,'col'=32] {'row'}, use_global_device_ids=true, to_apply=%region_13.0 | all-reduce | flops 64 | bytes 512 | tf_op jit(solution)/shard_map/psum | solution.py:28
  831.1 1.3 multiply_add_fusion
  (15 shorter events, 0.1 us)
Async XLA Ops:
  6.5 163.0 %all-reduce.5.cloned.1.call-start = ((), (), s32[]{:S(2)}) async-start(), calls=%async_computation | async-start | bytes 1966080 | tf_op jit(solution)/shard_map/psum | solution.py:35
  47.3 360.5 %copy-start.2 = (f32[64,256]{1,0:T(8,128)S(1)}, f32[64,256]{1,0:T(8,128)}, u32[]{:S(2)}) copy-start(f32[64,256]{1,0:T(8,128)} %param.3) | copy-start | bytes 196612
  47.3 360.5 %all-reduce.7.cloned.1.call-start = ((), (), s32[]{:S(2)}) async-start(), calls=%async_computation.1 | async-start | bytes 131072 | tf_op jit(solution)/shard_map/psum | solution.py:40
  226.2 332.1 %copy-start = (f32[64,3840]{1,0:T(8,128)S(1)}, f32[64,3840]{1,0:T(8,128)}, u32[]{:S(2)}) copy-start(f32[64,3840]{1,0:T(8,128)} %all-reduce.5.cloned.1.call-done) | copy-start | bytes 2949124
  226.2 332.1 %all-reduce.9.cloned.1.call-start = ((), (), s32[]{:S(2)}) async-start(), calls=%async_computation.2 | async-start | bytes 1966080 | tf_op jit(solution)/shard_map/psum | solution.py:35
  447.6 349.4 %all-reduce.11.cloned.1.call-start = ((), (), s32[]{:S(2)}) async-start(), calls=%async_computation.3 | async-start | bytes 131072 | tf_op jit(solution)/shard_map/psum | solution.py:40
  559.8 271.3 %copy-start.1 = (f32[64,3840]{1,0:T(8,128)S(1)}, f32[64,3840]{1,0:T(8,128)}, u32[]{:S(2)}) copy-start(f32[64,3840]{1,0:T(8,128)} %all-reduce.9.cloned.1.call-done) | copy-start | bytes 2949124
Sparse Core Ops, SparseCore 0:
  47.5 122.0 all-reduce.4
  226.3 181.4 all-reduce.6
  447.7 110.5 all-reduce.8
  615.4 181.4 all-reduce.10
where the time goes:
time: 844 us; the launch traced here: 839 us
  waiting for transfers between devices  596 us (71%)
  blocking collectives  198 us (23%)
  matrix products  24.6 us (3%)
  between operations  13.2 us (2%)
    psum x2, waiting for transfers between devices, forward_step(): forward_out = lax.psum(forward_product(right_raw / v_norm[:, None]), 'col')  363 us
    psum x2, waiting for transfers between devices, back_step(): back_out = lax.psum(back_product(left_raw / u_norm[:, None]), 'row')  233 us
    psum x3, blocking collectives, row_norm(): return jnp.sqrt(lax.psum(squares(left_raw), 'row'))  101 us
    psum x2, blocking collectives, col_norm(): return jnp.sqrt(lax.psum(squares(right_full), 'col'))  97.2 us
  transfers between devices with their start and end apart: 4, of which 4 were waited for; matrix products, arithmetic and copies ran while one was open for 0% of the time, Pallas kernels for 0%

commit v1 on v0

v1 whole, which is shorter than its diff:
```python
import jax
import jax.numpy as jnp
from jax import lax
from jax.experimental import pallas as pl
from jax.experimental.pallas import tpu as pltpu
from jax.sharding import PartitionSpec as P

MESH = pl.DeviceIdType.MESH
F32 = jnp.float32
BF16 = jnp.bfloat16
SETS = 64
DEPTH = 256
COLS = 3840
TILES = 15
STEPS = COLS // DEPTH


def split(x):
    high = x.astype(BF16)
    low = (x - high.astype(F32)).astype(BF16)
    return high, low


def lane_sum(x):
    return jnp.broadcast_to(jnp.sum(x, axis=-1, keepdims=True), x.shape)


def kernel(
    design, targets, out,
    raw, high, low, partial, arrived, right, units, line_out, line_in, left,
    row_norm, small_src, small_core, small_xy, small_z, tile_core, coef,
    load_sem, send_sem, recv_sem,
):
    me = lax.axis_index("row")
    col = lax.axis_index("col")
    depth_z = col // 2
    core = col % 2
    group = lax.rem(me, 8)
    line_group = lax.rem(depth_z, 8)

    plane = [{"row": lax.rem(me + k, 16), "col": col} for k in range(1, 16)]
    line = [{"row": me, "col": lax.rem(col + 2 * k, 32)} for k in range(1, 16)]
    twin = {"row": me, "col": depth_z * 2 + 1 - core}

    def send(src, dst, index, to):
        pltpu.make_async_remote_copy(
            src_ref=src, dst_ref=dst, send_sem=send_sem.at[index], recv_sem=recv_sem.at[index],
            device_id=to, device_id_type=MESH,
        ).start()

    def arrive(ref, index):
        pltpu.make_async_copy(ref, ref, recv_sem.at[index]).wait()

    def sent(ref, index):
        pltpu.make_async_copy(ref, ref, send_sem.at[index]).wait()

    def load(k):
        where = pl.ds(k * DEPTH, DEPTH)
        return pltpu.make_async_copy(design.at[:, where], raw.at[:, where], load_sem.at[k])

    for k in range(STEPS):
        load(k).start()
    barrier = pltpu.get_barrier_semaphore()
    for to in plane + line + [twin]:
        pl.semaphore_signal(barrier, inc=1, device_id=to, device_id_type=MESH)

    sets_row = lax.broadcasted_iota(jnp.int32, (SETS, 128), 0)
    sets_lane = lax.broadcasted_iota(jnp.int32, (SETS, 128), 1)
    diagonal = sets_row == sets_lane
    b = targets[...]
    squares = jnp.sum(b * b, axis=1, keepdims=True)
    as_row = jnp.sum(jnp.where(diagonal, jnp.broadcast_to(squares, (SETS, 128)), 0.0), axis=0, keepdims=True)
    row_norm[me] = jnp.broadcast_to(as_row, (8, 128))
    pl.semaphore_wait(barrier, 31)
    for to in plane:
        send(row_norm.at[me], row_norm.at[me], 0, to)

    for k in range(STEPS):
        load(k).wait()
        where = pl.ds(k * DEPTH, DEPTH)
        d_high, d_low = split(raw[:, where])
        high[:, where] = d_high
        low[:, where] = d_low

    arrive(row_norm.at[pl.ds(0, 15)], 0)
    sent(row_norm.at[pl.ds(0, 15)], 0)
    total = row_norm[0]
    for k in range(1, 16):
        total = total + row_norm[k]
    b_norm = jnp.sum(jnp.where(diagonal, jnp.broadcast_to(total[:1], (SETS, 128)), 0.0), axis=1, keepdims=True)
    b_norm = jnp.sqrt(jnp.broadcast_to(b_norm, (SETS, 128)))
    u_now = [b[:, :128] / b_norm, b[:, 128:] / b_norm]
    for half in range(2):
        units[pl.ds(8 * half, 8)] = u_now[half].reshape(8, 8, 128)

    def back(halves, turn):
        x_high, x_low = split(jnp.concatenate(halves, axis=1))
        both = jnp.concatenate([x_high, x_low], axis=0)
        for k in range(STEPS):
            where = pl.ds(k * DEPTH, DEPTH)
            first = jnp.dot(both, high[:, where], preferred_element_type=F32)
            second = jnp.dot(x_high, low[:, where], preferred_element_type=F32)
            result = first[:SETS] + (first[SETS:] + second)
            for i in range(2):
                h, j = divmod(2 * k + i, TILES)
                partial[pl.ds(8 * h, 8), j] = result[:, 128 * i:128 * (i + 1)].reshape(8, 8, 128)
        index = 1 + turn
        for to in plane:
            send(partial.at[to["row"]], arrived.at[turn, me], index, to)
        arrived[turn, me] = partial[me]
        arrive(arrived.at[turn, pl.ds(0, 15)], index)
        sent(arrived.at[turn, pl.ds(0, 15)], index)
        total = arrived[turn, 0]
        for k in range(1, 16):
            total = total + arrived[turn, k]
        return total

    def gather(piece, turn):
        right[turn, me] = piece
        index = 3 + turn
        for to in plane:
            send(right.at[turn, me], right.at[turn, me], index, to)
        base = 5 + 3 * turn
        small_z[turn, depth_z] = lane_sum(jnp.sum(piece * piece, axis=0))
        for to in line:
            send(small_z.at[turn, depth_z], small_z.at[turn, depth_z], base, to)
        arrive(small_z.at[turn, pl.ds(0, 15)], base)
        sent(small_z.at[turn, pl.ds(0, 15)], base)
        total = small_z[turn, 0]
        for k in range(1, 16):
            total = total + small_z[turn, k]
        small_src[turn] = total
        send(small_src.at[turn], small_core.at[turn], base + 1, twin)
        arrive(small_core.at[turn], base + 1)
        sent(small_core.at[turn], base + 1)
        small_xy[turn, me] = total + small_core[turn]
        for to in plane:
            send(small_xy.at[turn, me], small_xy.at[turn, me], base + 2, to)
        arrive(right.at[turn, pl.ds(0, 15)], index)
        sent(right.at[turn, pl.ds(0, 15)], index)

    def forward(turn):
        base = 5 + 3 * turn
        slabs = []
        for j in range(2 * TILES):
            h, i = divmod(j, TILES)
            slabs.append((pl.ds(8 * h, 8), i))
        squares = jnp.zeros((8, 8, 128), F32)
        for h, i in slabs:
            v = right[turn, h, i]
            squares = squares + v * v
        own = jnp.sqrt(lane_sum(squares))
        own = jnp.where(own > 0.0, own, 1.0)
        inverse = 1.0 / own
        first = jnp.zeros((2 * SETS, DEPTH), F32)
        second = jnp.zeros((SETS, DEPTH), F32)
        contract = (((1,), (1,)), ((), ()))
        for k in range(STEPS):
            where = pl.ds(k * DEPTH, DEPTH)
            w = [(right[turn, h, i] * inverse).reshape(SETS, 128) for h, i in slabs[2 * k:2 * k + 2]]
            w_high, w_low = split(jnp.concatenate(w, axis=1))
            both = jnp.concatenate([w_high, w_low], axis=0)
            first = first + lax.dot_general(both, high[:, where], contract, preferred_element_type=F32)
            second = second + lax.dot_general(w_high, low[:, where], contract, preferred_element_type=F32)
        result = first[:SETS] + (first[SETS:] + second)
        arrive(small_xy.at[turn, pl.ds(0, 15)], base + 2)
        sent(small_xy.at[turn, pl.ds(0, 15)], base + 2)
        v_norm = jnp.sqrt(small_xy[turn, pl.ds(0, 8)] + small_xy[turn, pl.ds(8, 8)])
        scale = own / v_norm
        for half in range(2):
            line_out[turn, pl.ds(8 * half, 8)] = result[:, 128 * half:128 * (half + 1)].reshape(8, 8, 128) * scale
        index = 11 + 2 * turn
        for to in line:
            send(line_out.at[turn, to["col"] // 2], line_in.at[turn, depth_z], index, to)
        line_in[turn, depth_z] = line_out[turn, depth_z]
        arrive(line_in.at[turn, pl.ds(0, 15)], index)
        sent(line_in.at[turn, pl.ds(0, 15)], index)
        total = line_in[turn, 0]
        for k in range(1, 16):
            total = total + line_in[turn, k]
        small_src[2 + turn] = total
        send(small_src.at[2 + turn], tile_core.at[turn], index + 1, twin)
        arrive(tile_core.at[turn], index + 1)
        sent(tile_core.at[turn], index + 1)
        return total + tile_core[turn], v_norm

    def start_norm(tile, turn):
        index = 15 + 2 * turn
        small_xy[2 + turn, me] = lane_sum(tile * tile)
        for to in plane:
            send(small_xy.at[2 + turn, me], small_xy.at[2 + turn, me], index, to)

    def middle_norm(turn):
        index = 15 + 2 * turn
        arrive(small_xy.at[2 + turn, pl.ds(0, 15)], index)
        sent(small_xy.at[2 + turn, pl.ds(0, 15)], index)
        total = small_xy[2 + turn, 0]
        for k in range(1, 16):
            total = total + small_xy[2 + turn, k]
        small_z[2 + turn, depth_z] = total
        for to in line:
            send(small_z.at[2 + turn, depth_z], small_z.at[2 + turn, depth_z], index + 1, to)

    def end_norm(turn):
        index = 15 + 2 * turn
        arrive(small_z.at[2 + turn, pl.ds(0, 15)], index + 1)
        sent(small_z.at[2 + turn, pl.ds(0, 15)], index + 1)
        return jnp.sqrt(small_z[2 + turn, pl.ds(0, 8)] + small_z[2 + turn, pl.ds(8, 8)])

    piece = back(u_now, 0)
    gather(piece, 0)
    tile, v_first = forward(0)
    coef[0] = v_first
    tile = tile - coef[0, line_group] * units[depth_z]
    start_norm(tile, 0)
    left[depth_z] = tile
    for to in line:
        send(left.at[depth_z], left.at[depth_z], 19, to)
    middle_norm(0)
    arrive(left.at[pl.ds(0, 15)], 19)
    sent(left.at[pl.ds(0, 15)], 19)
    halves = [(left[pl.ds(8 * half, 8)] / v_first).reshape(SETS, 128) for half in range(2)]
    piece = back(halves, 1)
    u_first = end_norm(0)
    coef[1] = u_first
    v_own, u_own = coef[0, group], coef[1, group]
    piece = piece * (v_own / u_own) - right[0, me] * (u_own / v_own)
    gather(piece, 1)
    tile, v_second = forward(1)
    coef[2] = v_second
    tile = tile - coef[2, line_group] * (left[depth_z] / coef[1, line_group])
    start_norm(tile, 1)
    middle_norm(1)
    u_second = end_norm(1)

    phi_bar = b_norm.reshape(8, 8, 128)
    rho = jnp.sqrt(v_first * v_first + u_first * u_first)
    cosine = v_first / rho
    sine = u_first / rho
    step = cosine * phi_bar / rho
    phi_bar = sine * phi_bar
    rho_bar = -cosine * v_second
    turn_back = sine * v_second / rho
    rho = jnp.sqrt(rho_bar * rho_bar + u_second * u_second)
    step_second = (rho_bar / rho) * phi_bar / rho
    for_first = (step - step_second * turn_back) / v_first
    for_second = step_second / v_second
    for j in range(2 * TILES):
        h, i = divmod(j, TILES)
        h = pl.ds(8 * h, 8)
        value = right[0, h, i] * for_first + right[1, h, i] * for_second
        out[:, pl.ds(128 * j, 128)] = value.reshape(SETS, 128)


def local(design, targets):
    tile = (8, 128)
    return pl.pallas_call(
        kernel,
        out_shape=jax.ShapeDtypeStruct((SETS, COLS), F32),
        in_specs=[pl.BlockSpec(memory_space=pl.ANY), pl.BlockSpec(memory_space=pltpu.VMEM)],
        out_specs=pl.BlockSpec(memory_space=pltpu.VMEM),
        scratch_shapes=[
            pltpu.VMEM((DEPTH, COLS), F32),
            pltpu.VMEM((DEPTH, COLS), BF16),
            pltpu.VMEM((DEPTH, COLS), BF16),
            pltpu.VMEM((16, TILES) + tile, F32),
            pltpu.VMEM((2, 16, TILES) + tile, F32),
            pltpu.VMEM((2, 16, TILES) + tile, F32),
            pltpu.VMEM((16,) + tile, F32),
            pltpu.VMEM((2, 16) + tile, F32),
            pltpu.VMEM((2, 16) + tile, F32),
            pltpu.VMEM((16,) + tile, F32),
            pltpu.VMEM((16,) + tile, F32),
            pltpu.VMEM((4,) + tile, F32),
            pltpu.VMEM((2,) + tile, F32),
            pltpu.VMEM((4, 16) + tile, F32),
            pltpu.VMEM((4, 16) + tile, F32),
            pltpu.VMEM((2,) + tile, F32),
            pltpu.VMEM((3, 8) + tile, F32),
            pltpu.SemaphoreType.DMA((STEPS,)),
            pltpu.SemaphoreType.DMA((20,)),
            pltpu.SemaphoreType.DMA((20,)),
        ],
        compiler_params=pltpu.CompilerParams(
            collective_id=0, has_side_effects=True, vmem_limit_bytes=48 << 20
        ),
    )(design, targets)


def solution(mesh):
    in_specs = (P("row", "col"), P(None, "row"))
    return jax.shard_map(local, mesh=mesh, in_specs=in_specs, out_specs=P(None, "col"), check_vma=False)
```

time: 844 us -> 130 us (0.15)
  waiting for transfers between devices: 596 us -> 0 us
  blocking collectives: 198 us -> 0 us
  Pallas kernels: 0 us -> 126 us
  matrix products: 24.6 us -> 0 us
  between operations: 13.2 us -> 0.01 us
    psum x4 -> x0, waiting for transfers between devices: 596 us -> none  [the longest x2 363 us: forward_step(): forward_out = lax.psum(forward_product(right_raw / v_norm[:, None]), 'col')]
    psum x5 -> x0, blocking collectives: 198 us -> none  [the longest x3 101 us: row_norm(): return jnp.sqrt(lax.psum(squares(left_raw), 'row'))]
    pallas_call x0 -> x1, Pallas kernels: none -> 126 us  [local(): pl.pallas_call(kernel, out_shape=jax.ShapeDtypeStruct((SETS, COLS), F32),...]
    dot_general x4 -> x0, matrix products: 24.6 us -> none  [the longest x2 13.5 us: forward_product(): lax.dot_general(vector, design, (((1,), (1,)), ((), ())), precision=highe...]
  transfers between devices with their start and end apart: 4 -> 0, of which waited for: 4 -> 0; matrix products, arithmetic and copies ran while one was open for 0% -> 0% of each run, Pallas kernels for 0% -> 0%
where the time goes in v1:
time: 130 us
  Pallas kernels  126 us (97%)
  local copies, waits for them, and re-layouts  3.9 us (3%)
    pallas_call x1, Pallas kernels, local(): pl.pallas_call(kernel, out_shape=jax.ShapeDtypeStruct((SETS, COLS), F32),...  126 us
    unnamed x5, local copies, waits for them, and re-layouts  3.9 us

profile of v1, /device:TPU:1, one launch (start us, length us, event | category | flops | bytes accessed | tf_op | source)
XLA Modules:
  0.0 130.0 jit_solution(3244850455989475359)
XLA Ops:
  0.0 0.0 copy-start
  0.0 2.1 %copy-done = f32[256,3840]{1,0:T(8,128)S(1)} copy-done((f32[256,3840]{1,0:T(8,128)S(1)}, f32[256,3840]{1,0:T(8,128)}, u32[]{:S(2)}) %copy-start) | copy-done | bytes 3932184
  2.1 0.0 copy-start.1
  2.1 0.8 copy-done.1
  3.0 126.1 %shard_map.28 = f32[64,3840]{1,0:T(8,128)S(1)} custom-call(f32[256,3840]{1,0:T(8,128)S(1)} %copy-done, f32[64,256]{1,0:T(8,128)S(1)} %copy-done.1), custom_call_target="tpu_custom_call" | custom-call | tf_op jit(solution)/shard_map/pallas_call | solution.py:257
  129.1 0.9 copy.4
Async XLA Ops:
  0.0 2.1 %copy-start = (f32[256,3840]{1,0:T(8,128)S(1)}, f32[256,3840]{1,0:T(8,128)}, u32[]{:S(2)}) copy-start(f32[256,3840]{1,0:T(8,128)} %design.1) | copy-start | bytes 11796484
  2.1 0.8 copy-start.1

commit v2 on v0

v2 whole, which is shorter than its diff:
```python
import jax
import jax.numpy as jnp
from jax import lax
from jax.experimental import pallas as pl
from jax.experimental.pallas import tpu as pltpu
from jax.sharding import PartitionSpec as P

MESH = pl.DeviceIdType.MESH
F32 = jnp.float32
BF16 = jnp.bfloat16
SETS = 64
HALF = 32
DEPTH = 256
COLS = 3840
TILES = 15
STEPS = COLS // DEPTH
FAR_FIRST = [(2, 2), (2, 1), (2, 3), (1, 2), (3, 2), (2, 0), (0, 2), (1, 1), (3, 3), (1, 3), (3, 1), (0, 1), (0, 3), (1, 0), (3, 0)]
LINE_EVEN = [8, 6, 10, 4, 12, 2, 14, 0]
LINE_ODD = [7, 9, 5, 11, 3, 13, 1, 15]


def split(x):
    high = x.astype(BF16)
    low = (x - high.astype(F32)).astype(BF16)
    return high, low


def lane_sum(x):
    return jnp.broadcast_to(jnp.sum(x, axis=-1, keepdims=True), x.shape)


def as_row(column):
    at = lax.broadcasted_iota(jnp.int32, (HALF, 128), 0) == lax.broadcasted_iota(jnp.int32, (HALF, 128), 1)
    return jnp.sum(jnp.where(at, column, 0.0), axis=0, keepdims=True)


def as_column(row):
    at = lax.broadcasted_iota(jnp.int32, (HALF, 128), 0) == lax.broadcasted_iota(jnp.int32, (HALF, 128), 1)
    return lane_sum(jnp.where(at, jnp.broadcast_to(row, (HALF, 128)), 0.0)).reshape(4, 8, 128)


def as_tile(row, group):
    sets = lax.broadcasted_iota(jnp.int32, (8, 128), 0) + 8 * group
    at = sets == lax.broadcasted_iota(jnp.int32, (8, 128), 1)
    return lane_sum(jnp.where(at, jnp.broadcast_to(row, (8, 128)), 0.0))


def positive(x):
    return jnp.where(x > 0.0, x, 1.0)


def kernel(
    design, targets, out,
    raw, high, low, base, partial, first_in, second_out, second_in, right, x_row, z_row, twin_out, twin_in, line_out, line_in,
    tile_out, tile_in, left, v_coef, u_coef, end_xy, end_z,
    load_sem, send_sem, recv_sem,
):
    me = lax.axis_index("row")
    col = lax.axis_index("col")
    x, y = me // 4, lax.rem(me, 4)
    z, core = col // 2, lax.rem(col, 2)
    z_parity = lax.rem(z, 2)
    my_tile = z_parity * 8 + z // 2
    tile_group = lax.rem(z // 2, 4)

    def in_plane(dx, dy):
        return lax.rem(x + dx, 4), lax.rem(y + dy, 4)

    def plane_id(tx, ty):
        return {"row": tx * 4 + ty, "col": col}

    plane = [plane_id(*in_plane(*d)) for d in FAR_FIRST]
    line = [
        {"row": me, "col": lax.rem(col + 2 * d, 32)}
        for d in (8, 7, 9, 6, 10, 5, 11, 4, 12, 3, 13, 2, 14, 1, 15)
    ]
    twin = {"row": me, "col": 2 * z + 1 - core}
    waits = []

    def send(src, dst, index, to):
        pltpu.make_async_remote_copy(
            src_ref=src, dst_ref=dst, send_sem=send_sem.at[index], recv_sem=recv_sem.at[index],
            device_id=to, device_id_type=MESH,
        ).start()

    def arrive(ref, index):
        pltpu.make_async_copy(ref, ref, recv_sem.at[index]).wait()

    def sent(ref, index, when=None):
        def wait():
            pltpu.make_async_copy(ref, ref, send_sem.at[index]).wait()
        waits.append((when, wait))

    def load(k):
        where = pl.ds(k * DEPTH, DEPTH)
        return pltpu.make_async_copy(design.at[:, where], raw.at[:, where], load_sem.at[k])

    fetch = pltpu.make_async_copy(targets, base, load_sem.at[STEPS])
    fetch.start()
    for k in range(STEPS):
        load(k).start()
    barrier = pltpu.get_barrier_semaphore()
    for to in plane + line + [twin]:
        pl.semaphore_signal(barrier, inc=1, device_id=to, device_id_type=MESH)

    def scaled(block, turn, groups):
        squares = jnp.broadcast_to(jnp.sum(block * block, axis=1, keepdims=True), (block.shape[0], 128))
        for i, g in enumerate(groups):
            x_row[turn, g, me] = as_row(squares[HALF * i:HALF * (i + 1)])
        norm = positive(jnp.sqrt(squares))
        norm = jnp.concatenate([norm, norm], axis=1)
        x_high, x_low = split(block / norm)
        return x_high, jnp.concatenate([x_high, x_low], axis=0)

    def product(x_high, both, k, turn, groups):
        rows = x_high.shape[0]
        where = pl.ds(k * DEPTH, DEPTH)
        first = jnp.dot(both, high[:, where], preferred_element_type=F32)
        second = jnp.dot(x_high, low[:, where], preferred_element_type=F32)
        result = first[:rows] + (first[rows:] + second)
        for i in range(2):
            h, j = divmod(2 * k + i, TILES)
            for n, g in enumerate(groups):
                partial[turn, pl.ds(8 * g + 4 * h, 4), j] = (
                    result[HALF * n:HALF * (n + 1), 128 * i:128 * (i + 1)].reshape(4, 8, 128)
                )

    places = ((y, x), (x, y))

    def chunk(g, way, place):
        return 8 * g + 4 * (place // 2) + 2 * way + lax.rem(place, 2)

    def around(way, leg):
        found = []
        for d in (2, 1, 3):
            if (way == 0) == (leg == 0):
                tx, ty = x, lax.rem(y + d, 4)
                found.append((ty, plane_id(tx, ty)))
            else:
                tx, ty = lax.rem(x + d, 4), y
                found.append((tx, plane_id(tx, ty)))
        return found

    def index_of(turn, g, way, step):
        return 32 + ((turn * 2 + g) * 2 + way) * 4 + step

    def scatter(turn, g):
        index = 2 * turn + g
        for to in plane:
            send(x_row.at[turn, g, me], x_row.at[turn, g, me], index, to)
        sent(x_row.at[turn, g, pl.ds(0, 15)], index)
        for way in range(2):
            index = index_of(turn, g, way, 0)
            for place, to in around(way, 0):
                send(
                    partial.at[turn, chunk(g, way, place), pl.ds(0, TILES)],
                    first_in.at[turn, g, way, places[way][0], pl.ds(0, TILES)], index, to,
                )
            sent(first_in.at[turn, g, way, pl.ds(0, 3), pl.ds(0, TILES)], index)

    def middle(turn, g):
        arrive(x_row.at[turn, g, pl.ds(0, 15)], 2 * turn + g)
        left_norms(turn, g)
        for way in range(2):
            here, there = places[way]
            eight = 2 * way + lax.rem(here, 2)
            norm = u_coef[turn, 4 * g + eight]

            def weight(place):
                row = 4 * x + place if way == 0 else 4 * place + y
                return jnp.sqrt(as_tile(x_row[turn, g, row], eight)) / norm

            total = partial[turn, chunk(g, way, here), pl.ds(0, TILES)] * weight(here)
            others = [(place, weight(place)) for place, _ in around(way, 0)]
            arrive(first_in.at[turn, g, way, pl.ds(0, 3), pl.ds(0, TILES)], index_of(turn, g, way, 0))
            for place, scale in others:
                total = total + first_in[turn, g, way, place, pl.ds(0, TILES)] * scale
            second_out[turn, g, way, pl.ds(0, TILES)] = total
            second_out[turn, g, way, TILES] = jnp.zeros((8, 128), F32)
            index = index_of(turn, g, way, 1)
            for place, to in around(way, 1):
                send(
                    second_out.at[turn, g, way, pl.ds(4 * place, 4)],
                    second_in.at[turn, g, way, there], index, to,
                )
            sent(second_in.at[turn, g, way, pl.ds(0, 3)], index)

    def spread(turn, g):
        for way in range(2):
            here, there = places[way]
            mine = pl.ds(4 * there, 4)
            which = chunk(g, way, here)
            eight = 4 * g + 2 * way + lax.rem(here, 2)
            total = second_out[turn, g, way, mine]
            if turn == 1:
                total = total - right[0, which, mine] * (u_coef[1, eight] / v_coef[0, eight])
            arrive(second_in.at[turn, g, way, pl.ds(0, 3)], index_of(turn, g, way, 1))
            for place, _ in around(way, 1):
                total = total + second_in[turn, g, way, place]
            right[turn, which, mine] = total
            index = index_of(turn, g, way, 2)
            for _, to in around(way, 1):
                send(right.at[turn, which, mine], right.at[turn, which, mine], index, to)
            sent(right.at[turn, 0, pl.ds(0, 12)], index)

    def widen(turn, g):
        for way in range(2):
            here, _ = places[way]
            which = chunk(g, way, here)
            arrive(right.at[turn, 0, pl.ds(0, 12)], index_of(turn, g, way, 2))
            index = index_of(turn, g, way, 3)
            for _, to in around(way, 0):
                send(right.at[turn, which, pl.ds(0, TILES)], right.at[turn, which, pl.ds(0, TILES)], index, to)
            sent(right.at[turn, pl.ds(0, 3), pl.ds(0, TILES)], index)

    def left_norms(turn, g):
        total = x_row[turn, g, 0]
        for s in range(1, 16):
            total = total + x_row[turn, g, s]
        u_coef[turn, pl.ds(4 * g, 4)] = jnp.sqrt(as_column(total))

    def forward(turn, g):
        for way in range(2):
            arrive(right.at[turn, pl.ds(0, 3), pl.ds(0, TILES)], index_of(turn, g, way, 3))
        slabs = [(pl.ds(8 * g + 4 * (j // TILES), 4), j % TILES) for j in range(2 * TILES)]
        squares = jnp.zeros((4, 8, 128), F32)
        for h, i in slabs:
            v = right[turn, h, i]
            squares = squares + v * v
        squares = lane_sum(squares)
        z_row[turn, g, z] = as_row(squares.reshape(HALF, 128))
        index = 12 + 2 * turn + g
        for to in line:
            send(z_row.at[turn, g, z], z_row.at[turn, g, z], index, to)
        sent(z_row.at[turn, g, pl.ds(0, 15)], index)
        inverse = 1.0 / positive(jnp.sqrt(squares))
        first = jnp.zeros((2 * HALF, DEPTH), F32)
        second = jnp.zeros((HALF, DEPTH), F32)
        contract = (((1,), (1,)), ((), ()))
        for k in range(STEPS):
            where = pl.ds(k * DEPTH, DEPTH)
            w = [(right[turn, h, i] * inverse).reshape(HALF, 128) for h, i in slabs[2 * k:2 * k + 2]]
            w_high, w_low = split(jnp.concatenate(w, axis=1))
            both = jnp.concatenate([w_high, w_low], axis=0)
            first = first + lax.dot_general(both, high[:, where], contract, preferred_element_type=F32)
            second = second + lax.dot_general(w_high, low[:, where], contract, preferred_element_type=F32)
        result = first[:HALF] + (first[HALF:] + second)
        for n in range(2):
            line_out[turn, pl.ds(8 * g + 4 * n, 4)] = result[:, 128 * n:128 * (n + 1)].reshape(4, 8, 128)
        index = 16 + 2 * turn + g
        swap = lax.rem(z_parity + g, 2)
        for i in range(8):
            even, odd = LINE_EVEN[i], LINE_ODD[i]
            tz = lax.rem(z + even + (odd - even) * swap, 16)

            def push():
                send(
                    line_out.at[turn, 8 * g + tz // 2], line_in.at[turn, z], index,
                    {"row": me, "col": 2 * tz + core},
                )

            if i < 7:
                push()
            else:
                pl.when(swap == 1)(push)
        sent(line_in.at[turn, pl.ds(0, 7)], index, swap == 0)
        sent(line_in.at[turn, pl.ds(0, 8)], index, swap == 1)

        @pl.when(swap == 0)
        def _():
            line_in[turn, z] = line_out[turn, my_tile]

    def tile_sum(turn, g):
        mine = z_parity == g
        arrive(z_row.at[turn, g, pl.ds(0, 15)], 12 + 2 * turn + g)
        total = z_row[turn, g, 0]
        for s in range(1, 16):
            total = total + z_row[turn, g, s]
        twin_out[turn, g] = total
        index = 20 + 2 * turn + g
        send(twin_out.at[turn, g], twin_in.at[turn, g], index, twin)
        sent(twin_out.at[turn, g], index)

        @pl.when(mine)
        def _():
            weights = [jnp.sqrt(as_tile(z_row[turn, g, s], tile_group)) for s in range(16)]
            norm = positive(jnp.sqrt(as_tile(twin_out[turn, g], tile_group)))
            arrive(line_in.at[turn, pl.ds(0, 15)], 16 + 2 * turn + g)
            part = line_in[turn, 0] * (weights[0] / norm)
            for s in range(1, 16):
                part = part + line_in[turn, s] * (weights[s] / norm)
            tile_out[turn] = part
            send(tile_out.at[turn], tile_in.at[turn], 24 + turn, twin)
        sent(tile_out.at[turn], 24 + turn, mine)
        arrive(twin_in.at[turn, g], index)
        v_coef[turn, pl.ds(4 * g, 4)] = jnp.sqrt(as_column(twin_out[turn, g] + twin_in[turn, g]))

        @pl.when(mine)
        def _():
            own = jnp.sqrt(as_tile(twin_out[turn, g], tile_group))
            other = jnp.sqrt(as_tile(twin_in[turn, g], tile_group))
            v_norm = v_coef[turn, 4 * g + tile_group]
            if turn == 0:
                half = pl.ds(128 * (z // 8), 128)
                where = pl.ds(pl.multiple_of(HALF * g + 8 * tile_group, 8), 8)
                before = base[where, half]
            else:
                before = left[my_tile]
            unit = before / u_coef[turn, 4 * g + tile_group]
            arrive(tile_in.at[turn], 24 + turn)
            tile = tile_out[turn] * (own / v_norm) + tile_in[turn] * (other / v_norm) - v_norm * unit
            if turn == 0:
                left[my_tile] = tile
                for to in line:
                    send(left.at[my_tile], left.at[my_tile], 26 + g, to)
            else:
                end_xy[me] = lane_sum(tile * tile)
                for to in plane:
                    send(end_xy.at[me], end_xy.at[me], 28, to)
        if turn == 0:
            sent(left.at[pl.ds(0, 15)], 26 + g, mine)
        else:
            sent(end_xy.at[pl.ds(0, 15)], 28, mine)

    def back(g):
        pl.when(z_parity == g)(lambda: arrive(left.at[pl.ds(0, 7)], 26 + g))
        pl.when(z_parity != g)(lambda: arrive(left.at[pl.ds(0, 8)], 26 + g))
        block = [left[pl.ds(8 * g + 4 * n, 4)].reshape(HALF, 128) for n in range(2)]
        x_high, both = scaled(jnp.concatenate(block, axis=1), 1, [g])
        for k in range(STEPS):
            product(x_high, both, k, 1, [g])
        scatter(1, g)

    def tile_end(g):
        mine = z_parity == g

        @pl.when(mine)
        def _():
            arrive(end_xy.at[pl.ds(0, 15)], 28)
            total = end_xy[0]
            for s in range(1, 16):
                total = total + end_xy[s]
            end_z[my_tile] = total
            for to in line:
                send(end_z.at[my_tile], end_z.at[my_tile], 29 + g, to)
        sent(end_z.at[pl.ds(0, 15)], 29 + g, mine)

    def combine(g):
        pl.when(z_parity == g)(lambda: arrive(end_z.at[pl.ds(0, 7)], 29 + g))
        pl.when(z_parity != g)(lambda: arrive(end_z.at[pl.ds(0, 8)], 29 + g))
        where = pl.ds(4 * g, 4)
        phi_bar, u_first = u_coef[0, where], u_coef[1, where]
        v_first, v_second = v_coef[0, where], v_coef[1, where]
        u_second = jnp.sqrt(end_z[pl.ds(8 * g, 4)] + end_z[pl.ds(8 * g + 4, 4)])
        rho = jnp.sqrt(v_first * v_first + u_first * u_first)
        cosine, sine = v_first / rho, u_first / rho
        step = cosine * phi_bar / rho
        phi_bar = sine * phi_bar
        rho_bar = -cosine * v_second
        turn_back = sine * v_second / rho
        rho = jnp.sqrt(rho_bar * rho_bar + u_second * u_second)
        step_second = (rho_bar / rho) * phi_bar / rho
        for_first = (step - step_second * turn_back) / v_first
        for_second = step_second / v_second
        for j in range(2 * TILES):
            h, i = pl.ds(8 * g + 4 * (j // TILES), 4), j % TILES
            value = right[0, h, i] * for_first + right[1, h, i] * for_second
            out[pl.ds(HALF * g, HALF), pl.ds(128 * j, 128)] = value.reshape(HALF, 128)

    fetch.wait()
    x_high, both = scaled(base[...], 0, [0, 1])
    for k in range(STEPS):
        load(k).wait()
        where = pl.ds(k * DEPTH, DEPTH)
        d_high, d_low = split(raw[:, where])
        high[:, where] = d_high
        low[:, where] = d_low
        product(x_high, both, k, 0, [0, 1])
    pl.semaphore_wait(barrier, 31)
    for g in range(2):
        scatter(0, g)
    for step in (middle, spread, widen):
        for g in range(2):
            step(0, g)
    forward(0, 0)
    forward(0, 1)
    tile_sum(0, 0)
    tile_sum(0, 1)
    back(0)
    back(1)
    for step in (middle, spread, widen):
        for g in range(2):
            step(1, g)
    forward(1, 0)
    forward(1, 1)
    tile_sum(1, 0)
    tile_sum(1, 1)
    tile_end(0)
    tile_end(1)
    combine(0)
    combine(1)
    for when, wait in waits:
        if when is None:
            wait()
        else:
            pl.when(when)(wait)


def local(design, targets):
    tile = (8, 128)
    return pl.pallas_call(
        kernel,
        out_shape=jax.ShapeDtypeStruct((SETS, COLS), F32),
        in_specs=[pl.BlockSpec(memory_space=pltpu.HBM)] * 2,
        out_specs=pl.BlockSpec(memory_space=pltpu.VMEM),
        scratch_shapes=[
            pltpu.VMEM((DEPTH, COLS), F32),
            pltpu.VMEM((DEPTH, COLS), BF16),
            pltpu.VMEM((DEPTH, COLS), BF16),
            pltpu.VMEM((SETS, DEPTH), F32),
            pltpu.VMEM((2, 16, 16) + tile, F32),
            pltpu.VMEM((2, 2, 2, 4, 16) + tile, F32),
            pltpu.VMEM((2, 2, 2, 16) + tile, F32),
            pltpu.VMEM((2, 2, 2, 4, 4) + tile, F32),
            pltpu.VMEM((2, 16, 16) + tile, F32),
            pltpu.VMEM((2, 2, 16, 1, 128), F32),
            pltpu.VMEM((2, 2, 16, 1, 128), F32),
            pltpu.VMEM((2, 2, 1, 128), F32),
            pltpu.VMEM((2, 2, 1, 128), F32),
            pltpu.VMEM((2, 16) + tile, F32),
            pltpu.VMEM((2, 16) + tile, F32),
            pltpu.VMEM((2,) + tile, F32),
            pltpu.VMEM((2,) + tile, F32),
            pltpu.VMEM((16,) + tile, F32),
            pltpu.VMEM((2, 8) + tile, F32),
            pltpu.VMEM((2, 8) + tile, F32),
            pltpu.VMEM((16,) + tile, F32),
            pltpu.VMEM((16,) + tile, F32),
            pltpu.SemaphoreType.DMA((STEPS + 1,)),
            pltpu.SemaphoreType.DMA((64,)),
            pltpu.SemaphoreType.DMA((64,)),
        ],
        compiler_params=pltpu.CompilerParams(
            collective_id=0, has_side_effects=True, vmem_limit_bytes=61 << 20
        ),
    )(design, targets)


def solution(mesh):
    in_specs = (P("row", "col"), P(None, "row"))
    return jax.shard_map(local, mesh=mesh, in_specs=in_specs, out_specs=P(None, "col"), check_vma=False)
```

time: 844 us -> 99.1 us (0.12)
  waiting for transfers between devices: 596 us -> 0 us
  blocking collectives: 198 us -> 0 us
  Pallas kernels: 0 us -> 96.8 us
  matrix products: 24.6 us -> 0 us
  between operations: 13.2 us -> 0.01 us
    psum x4 -> x0, waiting for transfers between devices: 596 us -> none  [the longest x2 363 us: forward_step(): forward_out = lax.psum(forward_product(right_raw / v_norm[:, None]), 'col')]
    psum x5 -> x0, blocking collectives: 198 us -> none  [the longest x3 101 us: row_norm(): return jnp.sqrt(lax.psum(squares(left_raw), 'row'))]
    pallas_call x0 -> x1, Pallas kernels: none -> 96.8 us  [local(): pl.pallas_call(kernel, out_shape=jax.ShapeDtypeStruct((SETS, COLS), F32),...]
    dot_general x4 -> x0, matrix products: 24.6 us -> none  [the longest x2 13.5 us: forward_product(): lax.dot_general(vector, design, (((1,), (1,)), ((), ())), precision=highe...]
  transfers between devices with their start and end apart: 4 -> 0, of which waited for: 4 -> 0; matrix products, arithmetic and copies ran while one was open for 0% -> 0% of each run, Pallas kernels for 0% -> 0%
where the time goes in v2:
time: 99.1 us; the launch traced here: 99 us
  Pallas kernels  96.8 us (98%)
  local copies, waits for them, and re-layouts  2.21 us (2%)
    pallas_call x1, Pallas kernels, local(): pl.pallas_call(kernel, out_shape=jax.ShapeDtypeStruct((SETS, COLS), F32),...  96.8 us
    unnamed x1, local copies, waits for them, and re-layouts  2.21 us

profile of v2, /device:TPU:1, one launch (start us, length us, event | category | flops | bytes accessed | tf_op | source)
XLA Modules:
  0.0 99.0 jit_solution(11089190254282352417)
XLA Ops:
  0.0 96.8 %shard_map.28 = f32[64,3840]{1,0:T(8,128)} custom-call(f32[256,3840]{1,0:T(8,128)} %design.1, f32[64,256]{1,0:T(8,128)} %targets.1), custom_call_target="tpu_custom_call" | custom-call | tf_op jit(solution)/shard_map/pallas_call | solution.py:411
  96.8 2.2 %copy.4 = f32[64,3840]{1,0:T(8,128)} copy(f32[64,3840]{1,0:T(8,128)} %shard_map.28) | data formatting | bytes 1966080

commit v3 on v2

v3 whole, which is shorter than its diff:
```python
import jax
import jax.numpy as jnp
from jax import lax
from jax.experimental import pallas as pl
from jax.experimental.pallas import tpu as pltpu
from jax.sharding import PartitionSpec as P

MESH = pl.DeviceIdType.MESH
F32 = jnp.float32
BF16 = jnp.bfloat16
SETS = 64
HALF = 32
DEPTH = 256
COLS = 3840
TILES = 15
STEPS = COLS // DEPTH
FAR_FIRST = [(2, 2), (2, 1), (2, 3), (1, 2), (3, 2), (2, 0), (0, 2), (1, 1), (3, 3), (1, 3), (3, 1), (0, 1), (0, 3), (1, 0), (3, 0)]


def split(x):
    high = x.astype(BF16)
    low = (x - high.astype(F32)).astype(BF16)
    return high, low


def lane_sum(x):
    return jnp.broadcast_to(jnp.sum(x, axis=-1, keepdims=True), x.shape)


def as_row(column):
    at = lax.broadcasted_iota(jnp.int32, (HALF, 128), 0) == lax.broadcasted_iota(jnp.int32, (HALF, 128), 1)
    return jnp.sum(jnp.where(at, column, 0.0), axis=0, keepdims=True)


def as_column(row):
    at = lax.broadcasted_iota(jnp.int32, (HALF, 128), 0) == lax.broadcasted_iota(jnp.int32, (HALF, 128), 1)
    return lane_sum(jnp.where(at, jnp.broadcast_to(row, (HALF, 128)), 0.0)).reshape(4, 8, 128)


def as_tile(row, group):
    sets = lax.broadcasted_iota(jnp.int32, (8, 128), 0) + 8 * group
    at = sets == lax.broadcasted_iota(jnp.int32, (8, 128), 1)
    return lane_sum(jnp.where(at, jnp.broadcast_to(row, (8, 128)), 0.0))


def tile_row(tile, group):
    sets = lax.broadcasted_iota(jnp.int32, (8, 128), 0) + 8 * group
    at = sets == lax.broadcasted_iota(jnp.int32, (8, 128), 1)
    return jnp.sum(jnp.where(at, tile, 0.0), axis=0, keepdims=True)


def positive(x):
    return jnp.where(x > 0.0, x, 1.0)


def kernel(
    design, targets, out,
    raw, high, low, high_turned, low_turned, base, partial, first_in, second_in, right, z_row, twin_out, twin_in, line_out, line_in,
    halves, half_in, left, v_coef, u_coef, end_xy, end_z,
    load_sem, send_sem, recv_sem, greeting,
):
    me = lax.axis_index("row")
    col = lax.axis_index("col")
    x, y = me // 4, lax.rem(me, 4)
    z, core = col // 2, lax.rem(col, 2)
    firsts = ((8, 9), (12, 13))

    def owner(turn, g, k):
        return lax.rem(firsts[turn][g] + 2 * k, 16)

    def owned(turn, g):
        ahead = lax.rem(z + 16 - firsts[turn][g], 16)
        return (ahead < 8) & (lax.rem(ahead, 2) == 0), lax.rem(ahead // 2, 4)

    def in_plane(dx, dy):
        return lax.rem(x + dx, 4), lax.rem(y + dy, 4)

    def plane_id(tx, ty):
        return {"row": tx * 4 + ty, "col": col}

    plane = [plane_id(*in_plane(*d)) for d in FAR_FIRST]
    line = [
        {"row": me, "col": lax.rem(col + 2 * d, 32)}
        for d in (8, 7, 9, 6, 10, 5, 11, 4, 12, 3, 13, 2, 14, 1, 15)
    ]
    twin = {"row": me, "col": 2 * z + 1 - core}
    other_line = [{"row": me, "col": lax.rem(2 * (z + d) + 1 - core, 32)} for d in range(1, 16)]
    on_line = {d: {"row": me, "col": lax.rem(col + 2 * d, 32)} for d in (1, 2, 4, 12, 14, 15)}
    near = [plane_id(*in_plane(d, 0)) for d in (1, 2, 3)] + [plane_id(*in_plane(0, d)) for d in (1, 2, 3)]
    near = near + [on_line[d] for d in (1, 2, 14, 15)] + [twin]

    def greet(n, distance):
        for d in (distance, 16 - distance):
            pl.semaphore_signal(greeting.at[n], inc=1, device_id=on_line[d], device_id_type=MESH)

    def greeted(n):
        pl.semaphore_wait(greeting.at[n], 2)

    waits = []

    def send(src, dst, index, to):
        pltpu.make_async_remote_copy(
            src_ref=src, dst_ref=dst, send_sem=send_sem.at[index], recv_sem=recv_sem.at[index],
            device_id=to, device_id_type=MESH,
        ).start()

    def arrive(ref, index):
        pltpu.make_async_copy(ref, ref, recv_sem.at[index]).wait()

    def sent(ref, index, when=None):
        def wait():
            pltpu.make_async_copy(ref, ref, send_sem.at[index]).wait()
        waits.append((when, wait))

    def load(k):
        where = pl.ds(k * DEPTH, DEPTH)
        return pltpu.make_async_copy(design.at[:, where], raw.at[:, where], load_sem.at[k])

    fetch = pltpu.make_async_copy(targets, base, load_sem.at[STEPS])
    fetch.start()
    for k in range(STEPS):
        load(k).start()
    barrier = pltpu.get_barrier_semaphore()
    for to in near:
        pl.semaphore_signal(barrier, inc=1, device_id=to, device_id_type=MESH)

    def scaled(block, turn, groups):
        squares = jnp.broadcast_to(jnp.sum(block * block, axis=1, keepdims=True), (block.shape[0], 128))
        for i, g in enumerate(groups):
            for h in range(2):
                partial[turn, pl.ds(8 * g + 4 * h, 4), TILES] = squares[HALF * i:HALF * (i + 1)].reshape(4, 8, 128)
        norm = positive(jnp.sqrt(squares))
        norm = jnp.concatenate([norm, norm], axis=1)
        x_high, x_low = split(block / norm)
        return x_high, jnp.concatenate([x_high, x_low], axis=0)

    def product(x_high, both, k, turn, groups):
        rows = x_high.shape[0]
        where = pl.ds(k * DEPTH, DEPTH)
        first = jnp.dot(both, high[:, where], preferred_element_type=F32)
        second = jnp.dot(x_high, low[:, where], preferred_element_type=F32)
        result = first[:rows] + (first[rows:] + second)
        for i in range(2):
            h, j = divmod(2 * k + i, TILES)
            for n, g in enumerate(groups):
                partial[turn, pl.ds(8 * g + 4 * h, 4), j] = (
                    result[HALF * n:HALF * (n + 1), 128 * i:128 * (i + 1)].reshape(4, 8, 128)
                )

    places = ((y, x), (x, y))

    def chunk(g, way, place):
        return 8 * g + 4 * (place // 2) + 2 * way + lax.rem(place, 2)

    def around(way, leg):
        found = []
        for d in (2, 1, 3):
            if (way == 0) == (leg == 0):
                tx, ty = x, lax.rem(y + d, 4)
                found.append((ty, plane_id(tx, ty)))
            else:
                tx, ty = lax.rem(x + d, 4), y
                found.append((tx, plane_id(tx, ty)))
        return found

    def index_of(turn, g, way, step):
        return 64 + ((turn * 2 + g) * 2 + way) * 3 + step

    def scatter(turn, g):
        for way in range(2):
            index = index_of(turn, g, way, 0)
            for place, to in around(way, 0):
                send(
                    partial.at[turn, chunk(g, way, place)], first_in.at[turn, g, way, places[way][0]], index, to
                )
            sent(first_in.at[turn, g, way, pl.ds(0, 3)], index)

    def summed(parts):
        squares = [part[TILES] for part in parts]
        square = (squares[0] + squares[1]) + (squares[2] + squares[3])
        norm = jnp.sqrt(square)
        inverse = 1.0 / positive(norm)
        total = jnp.zeros((TILES, 8, 128), F32)
        for part, w in zip(parts, squares):
            total = total + part[pl.ds(0, TILES)] * (jnp.sqrt(w) * inverse)
        return total, square, norm

    def middle(turn, g):
        for way in range(2):
            here, there = places[way]
            which = chunk(g, way, here)
            arrive(first_in.at[turn, g, way, pl.ds(0, 3)], index_of(turn, g, way, 0))
            parts = [partial.at[turn, which]] + [first_in.at[turn, g, way, place] for place, _ in around(way, 0)]
            total, square, _ = summed(parts)
            second_in[turn, g, way, there, pl.ds(0, TILES)] = total
            second_in[turn, g, way, there, TILES] = square
            index = index_of(turn, g, way, 1)
            for _, to in around(way, 1):
                send(second_in.at[turn, g, way, there], second_in.at[turn, g, way, there], index, to)
            sent(second_in.at[turn, g, way, pl.ds(0, 3)], index)

    def spread(turn, g):
        for way in range(2):
            here, _ = places[way]
            which = chunk(g, way, here)
            arrive(second_in.at[turn, g, way, pl.ds(0, 3)], index_of(turn, g, way, 1))
            total, square, norm = summed([second_in.at[turn, g, way, place] for place in range(4)])
            if turn == 1:
                v_norm = v_coef[0, 4 * g + 2 * way + lax.rem(here, 2)]
                total = total - right[0, which, pl.ds(0, TILES)] * (norm / v_norm)
            right[turn, which, pl.ds(0, TILES)] = total
            right[turn, which, TILES] = square
            index = index_of(turn, g, way, 2)
            for _, to in around(way, 0):
                send(right.at[turn, which], right.at[turn, which], index, to)
            sent(right.at[turn, pl.ds(0, 3)], index)

    def forward(turn, g):
        for way in range(2):
            arrive(right.at[turn, pl.ds(0, 3)], index_of(turn, g, way, 2))
        u_coef[turn, pl.ds(4 * g, 4)] = jnp.sqrt(right[turn, pl.ds(8 * g, 4), TILES])
        slabs = [(pl.ds(8 * g + 4 * (j // TILES), 4), j % TILES) for j in range(2 * TILES)]
        squares = jnp.zeros((4, 8, 128), F32)
        for h, i in slabs:
            v = right[turn, h, i]
            squares = squares + v * v
        squares = lane_sum(squares)
        twin_out[turn, g] = as_row(squares.reshape(HALF, 128))
        send(twin_out.at[turn, g], twin_in.at[turn, g], 20 + 2 * turn + g, twin)
        sent(twin_out.at[turn, g], 20 + 2 * turn + g)
        inverse = 1.0 / positive(jnp.sqrt(squares))
        first = jnp.zeros((2 * HALF, DEPTH), F32)
        second = jnp.zeros((HALF, DEPTH), F32)
        for k in range(STEPS):
            where = pl.ds(k * DEPTH, DEPTH)
            w = [(right[turn, h, i] * inverse).reshape(HALF, 128) for h, i in slabs[2 * k:2 * k + 2]]
            w_high, w_low = split(jnp.concatenate(w, axis=1))
            both = jnp.concatenate([w_high, w_low], axis=0)
            first = first + jnp.dot(both, high_turned[where, :], preferred_element_type=F32)
            second = second + jnp.dot(w_high, low_turned[where, :], preferred_element_type=F32)
        result = first[:HALF] + (first[HALF:] + second)
        for n in range(2):
            halves[turn, g, n] = result[:, 128 * n:128 * (n + 1)].reshape(4, 8, 128)
        index = 24 + 2 * turn + g
        send(halves.at[turn, g, 1 - core], half_in.at[turn, g], index, twin)
        sent(half_in.at[turn, g], index)
        arrive(twin_in.at[turn, g], 20 + 2 * turn + g)
        z_row[turn, g, z] = twin_out[turn, g] + twin_in[turn, g]
        other = as_column(twin_in[turn, g])
        inverse = 1.0 / positive(jnp.sqrt(squares + other))
        own, other = jnp.sqrt(squares) * inverse, jnp.sqrt(other) * inverse
        for to in line:
            send(z_row.at[turn, g, z], z_row.at[turn, g, z], 12 + 2 * turn + g, to)
        sent(z_row.at[turn, g, pl.ds(0, 15)], 12 + 2 * turn + g)
        arrive(half_in.at[turn, g], index)
        line_out[turn, g] = halves[turn, g, core] * own + half_in[turn, g] * other
        index = 16 + 2 * turn + g
        mine, my_eight = owned(turn, g)
        for k in range(4):
            to = owner(turn, g, k)

            @pl.when(to != z)
            def _():
                send(line_out.at[turn, g, k], line_in.at[turn, g, z], index, {"row": me, "col": 2 * to + core})

        @pl.when(mine)
        def _():
            line_in[turn, g, z] = line_out[turn, g, my_eight]

        sent(line_in.at[turn, g, pl.ds(0, 3)], index, mine)
        sent(line_in.at[turn, g, pl.ds(0, 4)], index, jnp.logical_not(mine))

    def tile_sum(turn, g):
        mine, eight = owned(turn, g)
        arrive(z_row.at[turn, g, pl.ds(0, 15)], 12 + 2 * turn + g)
        total = z_row[turn, g, 0]
        for s in range(1, 16):
            total = total + z_row[turn, g, s]
        v_coef[turn, pl.ds(4 * g, 4)] = jnp.sqrt(as_column(total))

        @pl.when(mine)
        def _():
            v_norm = v_coef[turn, 4 * g + eight]
            inverse = 1.0 / v_norm
            weights = [jnp.sqrt(as_tile(z_row[turn, g, s], eight)) * inverse for s in range(16)]
            if turn == 0:
                where = pl.ds(pl.multiple_of(HALF * g + 8 * eight, 8), 8)
                before = base[where, pl.ds(pl.multiple_of(128 * core, 128), 128)]
            else:
                before = left[g, core, eight]
            before = before * (v_norm / u_coef[turn, 4 * g + eight])
            arrive(line_in.at[turn, g, pl.ds(0, 15)], 16 + 2 * turn + g)
            tile = line_in[turn, g, 0] * weights[0]
            for s in range(1, 16):
                tile = tile + line_in[turn, g, s] * weights[s]
            tile = tile - before
            if turn == 0:
                left[g, core, eight] = tile
                for to in line:
                    send(left.at[g, core, eight], left.at[g, core, eight], 28 + g, to)
            else:
                end_xy[g, me] = tile_row(lane_sum(tile * tile), eight)
                for to in plane:
                    send(end_xy.at[g, me], end_xy.at[g, me], 60 + g, to)
        if turn == 0:
            sent(line_in.at[0, g, pl.ds(0, 15)], 28 + g, mine)
        else:
            sent(end_xy.at[g, pl.ds(0, 15)], 60 + g, mine)

    def back(g):
        mine, _ = owned(0, g)
        pl.when(mine)(lambda: arrive(left.at[g, 0, pl.ds(0, 3)], 28 + g))
        pl.when(jnp.logical_not(mine))(lambda: arrive(left.at[g, 0], 28 + g))
        send(left.at[g, core], left.at[g, core], 30 + g, twin)
        sent(left.at[g, 0], 30 + g)
        arrive(left.at[g, 0], 30 + g)
        block = [left[g, n].reshape(HALF, 128) for n in range(2)]
        x_high, both = scaled(jnp.concatenate(block, axis=1), 1, [g])
        for k in range(STEPS):
            product(x_high, both, k, 1, [g])
        scatter(1, g)

    def tile_end(g):
        mine, eight = owned(1, g)

        @pl.when(mine)
        def _():
            arrive(end_xy.at[g, pl.ds(0, 15)], 60 + g)
            total = end_xy[g, 0]
            for s in range(1, 16):
                total = total + end_xy[g, s]
            end_z[g, core, eight] = total
            for to in line:
                send(end_z.at[g, core, eight], end_z.at[g, core, eight], 62 + g, to)
            for to in other_line + [twin]:
                send(end_z.at[g, core, eight], end_z.at[g, core, eight], 32 + g, to)
        sent(end_xy.at[g, pl.ds(0, 15)], 62 + g, mine)
        sent(end_xy.at[g], 32 + g, mine)

    def combine(g):
        mine, _ = owned(1, g)
        pl.when(mine)(lambda: arrive(end_z.at[g, 0, pl.ds(0, 3)], 62 + g))
        pl.when(jnp.logical_not(mine))(lambda: arrive(end_z.at[g, 0], 62 + g))
        arrive(end_z.at[g, 0], 32 + g)
        where = pl.ds(4 * g, 4)
        phi_bar, u_first = u_coef[0, where], u_coef[1, where]
        v_first, v_second = v_coef[0, where], v_coef[1, where]
        ends = [end_z[g, n, k] for n in range(2) for k in range(4)]
        total = ends[0]
        for end in ends[1:]:
            total = total + end
        u_second = jnp.sqrt(as_column(total))
        rho = jnp.sqrt(v_first * v_first + u_first * u_first)
        cosine, sine = v_first / rho, u_first / rho
        step = cosine * phi_bar / rho
        phi_bar = sine * phi_bar
        rho_bar = -cosine * v_second
        turn_back = sine * v_second / rho
        rho = jnp.sqrt(rho_bar * rho_bar + u_second * u_second)
        step_second = (rho_bar / rho) * phi_bar / rho
        for_first = (step - step_second * turn_back) / v_first
        for_second = step_second / v_second
        for j in range(2 * TILES):
            h, i = pl.ds(8 * g + 4 * (j // TILES), 4), j % TILES
            value = right[0, h, i] * for_first + right[1, h, i] * for_second
            out[pl.ds(HALF * g, HALF), pl.ds(128 * j, 128)] = value.reshape(HALF, 128)

    def turn_over(start, stop):
        for k in range(start, stop):
            where = pl.ds(k * DEPTH, DEPTH)
            d_high, d_low = split(jnp.transpose(raw[:, where]))
            high_turned[where, :] = d_high
            low_turned[where, :] = d_low

    fetch.wait()
    x_high, both = scaled(base[...], 0, [0, 1])
    for k in range(STEPS):
        load(k).wait()
        where = pl.ds(k * DEPTH, DEPTH)
        d_high, d_low = split(raw[:, where])
        high[:, where] = d_high
        low[:, where] = d_low
        product(x_high, both, k, 0, [0, 1])
    pl.semaphore_wait(barrier, 11)
    for g in range(2):
        scatter(0, g)
    greet(0, 2)
    turn_over(0, 5)
    for g in range(2):
        middle(0, g)
    greeted(0)
    greet(1, 4)
    turn_over(5, 10)
    for g in range(2):
        spread(0, g)
    turn_over(10, STEPS)
    greeted(1)
    forward(0, 0)
    forward(0, 1)
    tile_sum(0, 0)
    tile_sum(0, 1)
    back(0)
    back(1)
    for step in (middle, spread):
        for g in range(2):
            step(1, g)
    forward(1, 0)
    forward(1, 1)
    tile_sum(1, 0)
    tile_sum(1, 1)
    tile_end(0)
    tile_end(1)
    combine(0)
    combine(1)
    for when, wait in waits:
        if when is None:
            wait()
        else:
            pl.when(when)(wait)


def local(design, targets):
    tile = (8, 128)
    return pl.pallas_call(
        kernel,
        out_shape=jax.ShapeDtypeStruct((SETS, COLS), F32),
        in_specs=[pl.BlockSpec(memory_space=pltpu.HBM)] * 2,
        out_specs=pl.BlockSpec(memory_space=pltpu.VMEM),
        scratch_shapes=[
            pltpu.VMEM((DEPTH, COLS), F32),
            pltpu.VMEM((DEPTH, COLS), BF16),
            pltpu.VMEM((DEPTH, COLS), BF16),
            pltpu.VMEM((COLS, DEPTH), BF16),
            pltpu.VMEM((COLS, DEPTH), BF16),
            pltpu.VMEM((SETS, DEPTH), F32),
            pltpu.VMEM((2, 16, 16) + tile, F32),
            pltpu.VMEM((2, 2, 2, 4, 16) + tile, F32),
            pltpu.VMEM((2, 2, 2, 4, 16) + tile, F32),
            pltpu.VMEM((2, 16, 16) + tile, F32),
            pltpu.VMEM((2, 2, 16, 1, 128), F32),
            pltpu.VMEM((2, 2, 1, 128), F32),
            pltpu.VMEM((2, 2, 1, 128), F32),
            pltpu.VMEM((2, 2, 4) + tile, F32),
            pltpu.VMEM((2, 2, 16) + tile, F32),
            pltpu.VMEM((2, 2, 2, 4) + tile, F32),
            pltpu.VMEM((2, 2, 4) + tile, F32),
            pltpu.VMEM((2, 2, 4) + tile, F32),
            pltpu.VMEM((2, 8) + tile, F32),
            pltpu.VMEM((2, 8) + tile, F32),
            pltpu.VMEM((2, 16, 1, 128), F32),
            pltpu.VMEM((2, 2, 4, 1, 128), F32),
            pltpu.SemaphoreType.DMA((STEPS + 1,)),
            pltpu.SemaphoreType.DMA((88,)),
            pltpu.SemaphoreType.DMA((88,)),
            pltpu.SemaphoreType.REGULAR((2,)),
        ],
        compiler_params=pltpu.CompilerParams(
            collective_id=0, has_side_effects=True, vmem_limit_bytes=61 << 20
        ),
    )(design, targets)


def solution(mesh):
    in_specs = (P("row", "col"), P(None, "row"))
    return jax.shard_map(local, mesh=mesh, in_specs=in_specs, out_specs=P(None, "col"), check_vma=False)
```

time: 99.1 us -> 93.5 us (0.943)
  Pallas kernels: 96.8 us -> 91.2 us
    pallas_call x1, Pallas kernels: 96.8 us -> 91.2 us  [local(): pl.pallas_call(kernel, out_shape=jax.ShapeDtypeStruct((SETS, COLS), F32),...]
where the time goes in v3:
time: 93.5 us; the launch traced here: 93.4 us
  Pallas kernels  91.2 us (98%)
  local copies, waits for them, and re-layouts  2.21 us (2%)
    pallas_call x1, Pallas kernels, local(): pl.pallas_call(kernel, out_shape=jax.ShapeDtypeStruct((SETS, COLS), F32),...  91.2 us
    unnamed x1, local copies, waits for them, and re-layouts  2.21 us

profile of v3, /device:TPU:1, one launch (start us, length us, event | category | flops | bytes accessed | tf_op | source)
XLA Modules:
  0.0 93.4 jit_solution(18258980663081894783)
XLA Ops:
  0.0 91.2 %shard_map.28 = f32[64,3840]{1,0:T(8,128)} custom-call(f32[256,3840]{1,0:T(8,128)} %design.1, f32[64,256]{1,0:T(8,128)} %targets.1), custom_call_target="tpu_custom_call" | custom-call | tf_op jit(solution)/shard_map/pallas_call | solution.py:424
  91.2 2.2 %copy.4 = f32[64,3840]{1,0:T(8,128)} copy(f32[64,3840]{1,0:T(8,128)} %shard_map.28) | data formatting | bytes 1966080

commit v4 on v3

--- a/solution.py
+++ b/solution.py
@@ -63,7 +63,7 @@
     col = lax.axis_index("col")
     x, y = me // 4, lax.rem(me, 4)
     z, core = col // 2, lax.rem(col, 2)
-    firsts = ((8, 9), (12, 13))
+    firsts = ((4, 5), (12, 13))
 
     def owner(turn, g, k):
         return lax.rem(firsts[turn][g] + 2 * k, 16)

time: 93.5 us -> 92.5 us (0.989)
  Pallas kernels: 91.2 us -> 90.1 us
    pallas_call x1, Pallas kernels: 91.2 us -> 90.1 us  [local(): pl.pallas_call(kernel, out_shape=jax.ShapeDtypeStruct((SETS, COLS), F32),...]
where the time goes in v4:
time: 92.5 us; the launch traced here: 92.4 us
  Pallas kernels  90.1 us (97%)
  local copies, waits for them, and re-layouts  2.21 us (2%)
    pallas_call x1, Pallas kernels, local(): pl.pallas_call(kernel, out_shape=jax.ShapeDtypeStruct((SETS, COLS), F32),...  90.1 us
    unnamed x1, local copies, waits for them, and re-layouts  2.21 us

profile of v4, /device:TPU:1, one launch (start us, length us, event | category | flops | bytes accessed | tf_op | source)
XLA Modules:
  0.0 92.4 jit_solution(5248536165111121703)
XLA Ops:
  0.0 90.1 %shard_map.28 = f32[64,3840]{1,0:T(8,128)} custom-call(f32[256,3840]{1,0:T(8,128)} %design.1, f32[64,256]{1,0:T(8,128)} %targets.1), custom_call_target="tpu_custom_call" | custom-call | tf_op jit(solution)/shard_map/pallas_call | solution.py:424
  90.2 2.2 %copy.4 = f32[64,3840]{1,0:T(8,128)} copy(f32[64,3840]{1,0:T(8,128)} %shard_map.28) | data formatting | bytes 1966080

commit v5 on v4

--- a/solution.py
+++ b/solution.py
@@ -63,7 +63,7 @@
     col = lax.axis_index("col")
     x, y = me // 4, lax.rem(me, 4)
     z, core = col // 2, lax.rem(col, 2)
-    firsts = ((4, 5), (12, 13))
+    firsts = ((4, 5), (11, 12))
 
     def owner(turn, g, k):
         return lax.rem(firsts[turn][g] + 2 * k, 16)
@@ -116,19 +116,19 @@
         where = pl.ds(k * DEPTH, DEPTH)
         return pltpu.make_async_copy(design.at[:, where], raw.at[:, where], load_sem.at[k])
 
+    barrier = pltpu.get_barrier_semaphore()
+    for to in near:
+        pl.semaphore_signal(barrier, inc=1, device_id=to, device_id_type=MESH)
     fetch = pltpu.make_async_copy(targets, base, load_sem.at[STEPS])
     fetch.start()
     for k in range(STEPS):
         load(k).start()
-    barrier = pltpu.get_barrier_semaphore()
-    for to in near:
-        pl.semaphore_signal(barrier, inc=1, device_id=to, device_id_type=MESH)
 
     def scaled(block, turn, groups):
         squares = jnp.broadcast_to(jnp.sum(block * block, axis=1, keepdims=True), (block.shape[0], 128))
         for i, g in enumerate(groups):
             for h in range(2):
-                partial[turn, pl.ds(8 * g + 4 * h, 4), TILES] = squares[HALF * i:HALF * (i + 1)].reshape(4, 8, 128)
+                partial[turn, pl.ds(8 * g + 4 * h, 4), 0] = squares[HALF * i:HALF * (i + 1)].reshape(4, 8, 128)
         norm = positive(jnp.sqrt(squares))
         norm = jnp.concatenate([norm, norm], axis=1)
         x_high, x_low = split(block / norm)
@@ -143,7 +143,7 @@
         for i in range(2):
             h, j = divmod(2 * k + i, TILES)
             for n, g in enumerate(groups):
-                partial[turn, pl.ds(8 * g + 4 * h, 4), j] = (
+                partial[turn, pl.ds(8 * g + 4 * h, 4), j + 1] = (
                     result[HALF * n:HALF * (n + 1), 128 * i:128 * (i + 1)].reshape(4, 8, 128)
                 )
 
@@ -163,63 +163,77 @@
                 found.append((tx, plane_id(tx, ty)))
         return found
 
-    def index_of(turn, g, way, step):
-        return 64 + ((turn * 2 + g) * 2 + way) * 3 + step
+    def index_of(turn, g, way, step, part):
+        return 64 + (((turn * 2 + g) * 2 + way) * 3 + step) * 2 + part
+
+    parts = (pl.ds(0, 8), pl.ds(8, 8))
 
     def scatter(turn, g):
-        for way in range(2):
-            index = index_of(turn, g, way, 0)
-            for place, to in around(way, 0):
-                send(
-                    partial.at[turn, chunk(g, way, place)], first_in.at[turn, g, way, places[way][0]], index, to
-                )
-            sent(first_in.at[turn, g, way, pl.ds(0, 3)], index)
-
-    def summed(parts):
-        squares = [part[TILES] for part in parts]
+        for part, where in enumerate(parts):
+            for way in range(2):
+                here, _ = places[way]
+                index = index_of(turn, g, way, 0, part)
+                for place, to in around(way, 0):
+                    send(
+                        partial.at[turn, chunk(g, way, place), where],
+                        first_in.at[turn, g, way, here, where], index, to,
+                    )
+                sent(first_in.at[turn, g, way, pl.ds(0, 3), where], index)
+
+    def summed(refs, part):
+        squares = [ref[0] for ref in refs]
         square = (squares[0] + squares[1]) + (squares[2] + squares[3])
         norm = jnp.sqrt(square)
         inverse = 1.0 / positive(norm)
-        total = jnp.zeros((TILES, 8, 128), F32)
-        for part, w in zip(parts, squares):
-            total = total + part[pl.ds(0, TILES)] * (jnp.sqrt(w) * inverse)
-        return total, square, norm
+        weights = [jnp.sqrt(w) * inverse for w in squares]
+        where = pl.ds(1, 7) if part == 0 else pl.ds(8, 8)
+        total = refs[0][where] * weights[0]
+        for ref, weight in zip(refs[1:], weights[1:]):
+            total = total + ref[where] * weight
+        return total, square, norm, where
 
     def middle(turn, g):
-        for way in range(2):
-            here, there = places[way]
-            which = chunk(g, way, here)
-            arrive(first_in.at[turn, g, way, pl.ds(0, 3)], index_of(turn, g, way, 0))
-            parts = [partial.at[turn, which]] + [first_in.at[turn, g, way, place] for place, _ in around(way, 0)]
-            total, square, _ = summed(parts)
-            second_in[turn, g, way, there, pl.ds(0, TILES)] = total
-            second_in[turn, g, way, there, TILES] = square
-            index = index_of(turn, g, way, 1)
-            for _, to in around(way, 1):
-                send(second_in.at[turn, g, way, there], second_in.at[turn, g, way, there], index, to)
-            sent(second_in.at[turn, g, way, pl.ds(0, 3)], index)
+        for part in range(2):
+            for way in range(2):
+                here, there = places[way]
+                which = chunk(g, way, here)
+                arrive(first_in.at[turn, g, way, pl.ds(0, 3), parts[part]], index_of(turn, g, way, 0, part))
+                refs = [partial.at[turn, which]] + [first_in.at[turn, g, way, p] for p, _ in around(way, 0)]
+                total, square, _, where = summed(refs, part)
+                second_in[turn, g, way, there, where] = total
+                if part == 0:
+                    second_in[turn, g, way, there, 0] = square
+                index = index_of(turn, g, way, 1, part)
+                block = second_in.at[turn, g, way, there, parts[part]]
+                for _, to in around(way, 1):
+                    send(block, block, index, to)
+                sent(second_in.at[turn, g, way, pl.ds(0, 3), parts[part]], index)
 
     def spread(turn, g):
-        for way in range(2):
-            here, _ = places[way]
-            which = chunk(g, way, here)
-            arrive(second_in.at[turn, g, way, pl.ds(0, 3)], index_of(turn, g, way, 1))
-            total, square, norm = summed([second_in.at[turn, g, way, place] for place in range(4)])
-            if turn == 1:
-                v_norm = v_coef[0, 4 * g + 2 * way + lax.rem(here, 2)]
-                total = total - right[0, which, pl.ds(0, TILES)] * (norm / v_norm)
-            right[turn, which, pl.ds(0, TILES)] = total
-            right[turn, which, TILES] = square
-            index = index_of(turn, g, way, 2)
-            for _, to in around(way, 0):
-                send(right.at[turn, which], right.at[turn, which], index, to)
-            sent(right.at[turn, pl.ds(0, 3)], index)
+        for part in range(2):
+            for way in range(2):
+                here, _ = places[way]
+                which = chunk(g, way, here)
+                arrive(second_in.at[turn, g, way, pl.ds(0, 3), parts[part]], index_of(turn, g, way, 1, part))
+                total, square, norm, where = summed([second_in.at[turn, g, way, p] for p in range(4)], part)
+                if turn == 1:
+                    v_norm = v_coef[0, 4 * g + 2 * way + lax.rem(here, 2)]
+                    total = total - right[0, which, where] * (norm / v_norm)
+                right[turn, which, where] = total
+                if part == 0:
+                    right[turn, which, 0] = square
+                index = index_of(turn, g, way, 2, part)
+                block = right.at[turn, which, parts[part]]
+                for _, to in around(way, 0):
+                    send(block, block, index, to)
+                sent(right.at[turn, pl.ds(0, 3), parts[part]], index)
 
     def forward(turn, g):
         for way in range(2):
-            arrive(right.at[turn, pl.ds(0, 3)], index_of(turn, g, way, 2))
-        u_coef[turn, pl.ds(4 * g, 4)] = jnp.sqrt(right[turn, pl.ds(8 * g, 4), TILES])
-        slabs = [(pl.ds(8 * g + 4 * (j // TILES), 4), j % TILES) for j in range(2 * TILES)]
+            for part in range(2):
+                arrive(right.at[turn, pl.ds(0, 3), parts[part]], index_of(turn, g, way, 2, part))
+        u_coef[turn, pl.ds(4 * g, 4)] = jnp.sqrt(right[turn, pl.ds(8 * g, 4), 0])
+        slabs = [(pl.ds(8 * g + 4 * (j // TILES), 4), j % TILES + 1) for j in range(2 * TILES)]
         squares = jnp.zeros((4, 8, 128), F32)
         for h, i in slabs:
             v = right[turn, h, i]
@@ -361,7 +375,7 @@
         for_first = (step - step_second * turn_back) / v_first
         for_second = step_second / v_second
         for j in range(2 * TILES):
-            h, i = pl.ds(8 * g + 4 * (j // TILES), 4), j % TILES
+            h, i = pl.ds(8 * g + 4 * (j // TILES), 4), j % TILES + 1
             value = right[0, h, i] * for_first + right[1, h, i] * for_second
             out[pl.ds(HALF * g, HALF), pl.ds(128 * j, 128)] = value.reshape(HALF, 128)
 
@@ -450,8 +464,8 @@
             pltpu.VMEM((2, 16, 1, 128), F32),
             pltpu.VMEM((2, 2, 4, 1, 128), F32),
             pltpu.SemaphoreType.DMA((STEPS + 1,)),
-            pltpu.SemaphoreType.DMA((88,)),
-            pltpu.SemaphoreType.DMA((88,)),
+            pltpu.SemaphoreType.DMA((112,)),
+            pltpu.SemaphoreType.DMA((112,)),
             pltpu.SemaphoreType.REGULAR((2,)),
         ],
         compiler_params=pltpu.CompilerParams(

time: 92.5 us -> 91.7 us (level)
  no operation moved by 1% of the time
where the time goes in v5:
time: 91.7 us; the launch traced here: 91.6 us
  Pallas kernels  89.4 us (97%)
  local copies, waits for them, and re-layouts  2.21 us (2%)
    pallas_call x1, Pallas kernels, local(): pl.pallas_call(kernel, out_shape=jax.ShapeDtypeStruct((SETS, COLS), F32),...  89.4 us
    unnamed x1, local copies, waits for them, and re-layouts  2.21 us

profile of v5, /device:TPU:1, one launch (start us, length us, event | category | flops | bytes accessed | tf_op | source)
XLA Modules:
  0.0 91.6 jit_solution(7075616890468167591)
XLA Ops:
  0.0 89.4 %shard_map.28 = f32[64,3840]{1,0:T(8,128)} custom-call(f32[256,3840]{1,0:T(8,128)} %design.1, f32[64,256]{1,0:T(8,128)} %targets.1), custom_call_target="tpu_custom_call" | custom-call | tf_op jit(solution)/shard_map/pallas_call | solution.py:438
  89.4 2.2 %copy.4 = f32[64,3840]{1,0:T(8,128)} copy(f32[64,3840]{1,0:T(8,128)} %shard_map.28) | data formatting | bytes 1966080
